TPU v7x, 512 devices: a whole 4x8x8 slice. The times are simulated.
512 devices in a mesh: expert: 64 (over x, z, core), replica: 8 (over y).
Axes of the slice: x: 4, y: 8, z: 8, core: 2. Of those that a mesh axis runs over, the one named last changes fastest.
Arguments:
- tokens: bfloat16 [768, 3584], P('expert', 'replica'), may hold values from -6 to 6
- expert_ids: int32 [768, 8], P('expert'), may hold values from 0 to 31, all different within a row; in each aligned block of 12 rows (0 to 11, 12 to 23, ...) at most 4 rows name the same one
- gate_values: float32 [768, 8], P('expert'), may hold values from 0.1 to 0.6
- gate_weight: bfloat16 [64, 512, 3584], P('expert', 'replica'), may hold values from -0.09375 to 0.09375
- up_weight: bfloat16 [64, 512, 3584], P('expert', 'replica'), may hold values from -0.09375 to 0.09375
- down_weight: bfloat16 [64, 512, 3584], P('expert', None, 'replica'), may hold values from -0.1875 to 0.1875
- out_grad: bfloat16 [768, 3584], P('expert', 'replica'), may hold values from -1.5 to 1.5
Outputs:
- moe_out: bfloat16 [768, 3584], P('expert', 'replica')
- token_grad: bfloat16 [768, 3584], P('expert', 'replica')
- gate_grad: bfloat16 [64, 512, 3584], P('expert', 'replica')
- up_grad: bfloat16 [64, 512, 3584], P('expert', 'replica')
- down_grad: bfloat16 [64, 512, 3584], P('expert', None, 'replica')
Inputs may be any that keep to these rules, and one draw needn't show every extreme that they name: `expert_ids`: each row names 8 different experts. Among the 12 rows of one index of expert, no expert is named by more than 4 rows, a bound that some block reaches.
All inputs are finite; a program needn't handle non-finite values.
Results may differ from a plain program's by a relative error of at most 0.0075.
Values may be sent and summed in bfloat16 or wider, within the bound.
A program may use at most 64 MiB of HBM per device.

v0:
```python
import jax
import jax.numpy as jnp
from jax import lax
from jax.sharding import PartitionSpec as P


def partner_2(block, axis, distance):
    count = lax.axis_size(axis)
    route = []
    for low in range(count):
        high = low | 1 << distance
        if high != low and high < count:
            route += [(low, high), (high, low)]
    return lax.ppermute(block, axis, route)


def pair_join(parity_bit, own_part, peer_part, stack_axis):
    first_part = jnp.where(parity_bit == 0, own_part, peer_part)
    second_part = jnp.where(parity_bit == 0, peer_part, own_part)
    return jnp.stack([first_part, second_part], axis=stack_axis)


def pick_half(parity_bit, stacked, stack_axis):
    lower = jnp.take(stacked, 0, axis=stack_axis)
    higher = jnp.take(stacked, 1, axis=stack_axis)
    return (jnp.where(parity_bit == 0, lower, higher), jnp.where(parity_bit == 0, higher, lower))


def per_device(tokens, expert_ids, gate_values, gate_weight, up_weight, down_weight, out_grad):
    experts_axis = lax.axis_size("expert")
    tok_rows, slice_width = tokens.shape
    top_count = expert_ids.shape[1]
    expert_count = experts_axis // 2
    most_rows = min(tok_rows, 4 * tok_rows * top_count // (3 * expert_count))
    capacity = (most_rows + 1) // 2
    pair_count = tok_rows * top_count
    slot_count = experts_axis * capacity
    flat_ids = expert_ids.reshape(pair_count)
    onehot = (flat_ids[:, None] == jnp.arange(expert_count, dtype=jnp.int32)[None, :]).astype(
        jnp.int32
    )
    rank_in = jnp.sum((jnp.cumsum(onehot, axis=0) - onehot) * onehot, axis=1)
    upper_copy = (rank_in >= capacity).astype(jnp.int32)
    target = (2 * flat_ids + upper_copy) * capacity + rank_in - upper_copy * capacity
    slot_match = target[None, :] == jnp.arange(slot_count, dtype=jnp.int32)[:, None]
    filled = jnp.any(slot_match, axis=1)
    source_pair = jnp.sum(
        jnp.where(slot_match, jnp.arange(pair_count, dtype=jnp.int32)[None, :], 0), axis=1
    )
    source_token = source_pair // top_count
    flat_gates = gate_values.reshape(pair_count)
    send_rows = jnp.where(filled[:, None], tokens[source_token], jnp.zeros((), tokens.dtype))
    scaled = flat_gates[source_pair][:, None] * out_grad[source_token].astype(jnp.float32)
    send_grads = jnp.where(filled[:, None], scaled, 0.0).astype(jnp.bfloat16)
    got_rows, got_grads = (
        lax.all_to_all(
            send_rows.reshape(experts_axis, capacity, slice_width),
            "expert",
            split_axis=0,
            concat_axis=0,
            tiled=True,
        ),
        lax.all_to_all(
            send_grads.reshape(experts_axis, capacity, slice_width),
            "expert",
            split_axis=0,
            concat_axis=0,
            tiled=True,
        ),
    )
    rows_part = got_rows.reshape(slot_count, slice_width)
    grads_part = got_grads.reshape(slot_count, slice_width)
    parity_bit = lax.axis_index("expert") % 2
    own_pieces = (gate_weight[0], up_weight[0], down_weight[0])
    partner = partner_2((own_pieces[0], own_pieces[1], own_pieces[2]), "expert", 0)
    w_gate = pair_join(parity_bit, own_pieces[0], partner[0], 0)
    w_up = pair_join(parity_bit, own_pieces[1], partner[1], 0)
    w_down = pair_join(parity_bit, own_pieces[2], partner[2], 0)
    _, quarter, model_width = w_gate.shape
    full_rows = lax.all_gather(rows_part, "replica", axis=1, tiled=True)
    contract = (((1,), (1,)), ((), ()))
    pre_gate = lax.dot_general(
        full_rows,
        w_gate.reshape(2 * quarter, model_width),
        contract,
        preferred_element_type=jnp.float32,
    ).reshape(slot_count, 2, quarter)
    pre_up = lax.dot_general(
        full_rows,
        w_up.reshape(2 * quarter, model_width),
        contract,
        preferred_element_type=jnp.float32,
    ).reshape(slot_count, 2, quarter)
    sigma = jax.nn.sigmoid(pre_gate)
    activated = pre_gate * sigma
    slope_term = sigma * (1.0 + pre_gate * (1.0 - sigma))
    hidden = (activated * pre_up).astype(jnp.bfloat16)
    all_hidden = lax.all_gather(hidden, "replica", axis=2, tiled=True).reshape(slot_count, -1)
    down_full = w_down.reshape(-1, slice_width)
    expert_out = jnp.dot(all_hidden, down_full, preferred_element_type=jnp.float32).astype(
        jnp.bfloat16
    )
    returned = lax.all_to_all(
        expert_out.reshape(experts_axis, capacity, slice_width),
        "expert",
        split_axis=0,
        concat_axis=0,
        tiled=True,
    ).reshape(slot_count, slice_width)
    picked = returned[target].astype(jnp.float32).reshape(tok_rows, top_count, slice_width)
    moe_out = jnp.sum(picked * gate_values[:, :, None], axis=1).astype(jnp.bfloat16)
    down_local = lax.dot_general(
        all_hidden, grads_part, (((0,), (0,)), ((), ())), preferred_element_type=jnp.float32
    )
    full_grads = lax.all_gather(grads_part, "replica", axis=1, tiled=True)
    down_rows = lax.all_to_all(w_down, "replica", split_axis=1, concat_axis=2, tiled=True)
    hidden_grad = jnp.einsum(
        "sd,hqd->shq", full_grads, down_rows, preferred_element_type=jnp.float32
    )
    gate_act = (hidden_grad * pre_up * slope_term).astype(jnp.bfloat16)
    up_act = (hidden_grad * activated).astype(jnp.bfloat16)
    gate_local = jnp.einsum("sd,shq->hqd", full_rows, gate_act, preferred_element_type=jnp.float32)
    up_local = jnp.einsum("sd,shq->hqd", full_rows, up_act, preferred_element_type=jnp.float32)
    all_gate_act, all_up_act = (
        lax.all_gather(gate_act, "replica", axis=2, tiled=True),
        lax.all_gather(up_act, "replica", axis=2, tiled=True),
    )
    rows_gate, rows_up = (
        lax.all_to_all(w_gate, "replica", split_axis=2, concat_axis=1, tiled=True),
        lax.all_to_all(w_up, "replica", split_axis=2, concat_axis=1, tiled=True),
    )
    input_rows = jnp.einsum(
        "shf,hfd->sd", all_gate_act, rows_gate, preferred_element_type=jnp.float32
    )
    input_rows = input_rows + jnp.einsum(
        "shf,hfd->sd", all_up_act, rows_up, preferred_element_type=jnp.float32
    )
    grads_back = lax.all_to_all(
        input_rows.astype(jnp.bfloat16).reshape(experts_axis, capacity, slice_width),
        "expert",
        split_axis=0,
        concat_axis=0,
        tiled=True,
    ).reshape(slot_count, slice_width)
    token_grad = jnp.sum(
        grads_back[target].astype(jnp.float32).reshape(tok_rows, top_count, slice_width), axis=1
    ).astype(jnp.bfloat16)
    keep_gate, give_gate = pick_half(parity_bit, gate_local, 0)
    keep_up, give_up = pick_half(parity_bit, up_local, 0)
    keep_down, give_down = pick_half(parity_bit, down_local.reshape(2, -1, slice_width), 0)
    received = (
        partner_2(give_gate.astype(jnp.bfloat16), "expert", 0).astype(give_gate.dtype),
        partner_2(give_up.astype(jnp.bfloat16), "expert", 0).astype(give_up.dtype),
        partner_2(give_down.astype(jnp.bfloat16), "expert", 0).astype(give_down.dtype),
    )
    gate_grad = (keep_gate + received[0]).astype(jnp.bfloat16)[None]
    up_grad = (keep_up + received[1]).astype(jnp.bfloat16)[None]
    down_grad = (keep_down + received[2]).astype(jnp.bfloat16)[None]
    return (moe_out, token_grad, gate_grad, up_grad, down_grad)


def solution(mesh):
    placed = (
        P("expert", "replica"),
        P("expert", None),
        P("expert", None),
        P("expert", "replica", None),
        P("expert", "replica", None),
        P("expert", None, "replica"),
        P("expert", "replica"),
    )
    return jax.shard_map(
        per_device,
        mesh=mesh,
        in_specs=placed,
        out_specs=(
            P("expert", "replica"),
            P("expert", "replica"),
            P("expert", "replica", None),
            P("expert", "replica", None),
            P("expert", None, "replica"),
        ),
        check_vma=False,
    )
```

profile of v0, /device:TPU:1, one launch (start us, length us, event | category | flops | bytes accessed | tf_op | source)
XLA Modules:
  0.0 322.7 jit_solution(3056633494185465903)
XLA Ops:
  0.7 8.9 %collective-permute-start.2 = (bf16[512,448]{0,1:T(8,128)(2,1)}, bf16[512,448]{0,1:T(8,128)(2,1)S(1)}, u32[]{:S(2)}, u32[]{:S(2)}) collective-permute-start(bf16[512,448]{0,1:T(8,128)(2,1)} %bitcast.169), channel_id=1, source_target_pairs={{0,8},{8,0},{16,24},{24,16},{32,40},{40,32},{48,56},{56,48},{64,72... | collective-permute-start | bytes 1376264 | tf_op jit(solution)/shard_map/ppermute | solution.py:14
  9.6 0.8 copy.56
  11.1 0.8 gather_fusion.3
  12.3 0.8 copy.60
  13.2 0.5 copy-done.18
  13.7 1.2 gather_fusion.2
  15.1 0.9 select_convert_fusion.3
  15.9 8.1 %all-to-all-start.2 = ((bf16[64,2,448]{2,1,0:T(2,128)(2,1)}), bf16[64,2,448]{2,1,0:T(2,128)(2,1)S(1)}, u32[]{:S(2)}, u32[]{:S(2)}) async-start(bf16[64,2,448]{2,1,0:T(2,128)(2,1)} %select_convert_fusion.3), calls=%async_computation.2 | async-start | bytes 262144 | tf_op jit(solution)/shard_map/all_to_all | solution.py:63
  24.0 2.4 collective-permute-start.1
  26.4 2.0 collective-permute-start
  28.4 0.8 gather_fusion
  29.5 0.9 broadcast_select_fusion
  30.4 4.0 %all-to-all-done.2 = bf16[64,2,448]{2,1,0:T(2,128)(2,1)S(1)} async-done(((bf16[64,2,448]{2,1,0:T(2,128)(2,1)}), bf16[64,2,448]{2,1,0:T(2,128)(2,1)S(1)}, u32[]{:S(2)}, u32[]{:S(2)}) %all-to-all-start.2) | async-done | bytes 114720 | tf_op jit(solution)/shard_map/all_to_all | solution.py:63
  34.4 6.3 %all-to-all-start = ((bf16[64,2,448]{2,1,0:T(2,128)(2,1)}), bf16[64,2,448]{2,1,0:T(2,128)(2,1)S(1)}, u32[]{:S(2)}, u32[]{:S(2)}) async-start(bf16[64,2,448]{2,1,0:T(2,128)(2,1)} %broadcast_select_fusion), calls=%async_computation | async-start | bytes 262144 | tf_op jit(solution)/shard_map/all_to_all | solution.py:56
  40.7 0.6 pad_clamp_fusion.1
  41.6 9.5 %all-to-all-done = bf16[64,2,448]{2,1,0:T(2,128)(2,1)S(1)} async-done(((bf16[64,2,448]{2,1,0:T(2,128)(2,1)}), bf16[64,2,448]{2,1,0:T(2,128)(2,1)S(1)}, u32[]{:S(2)}, u32[]{:S(2)}) %all-to-all-start) | async-done | bytes 114720 | tf_op jit(solution)/shard_map/all_to_all | solution.py:56
  51.3 24.1 %all_gather.17 = bf16[128,3584]{0,1:T(8,128)(2,1)} all-gather(bf16[128,448]{0,1:T(8,128)(2,1)S(1)} %copy.62), channel_id=1, replica_groups=mesh['expert'=64,'replica'=8] {'replica'}, dimensions={1}, use_global_device_ids=true | all-gather | bytes 1032192 | tf_op jit(solution)/shard_map/all_gather | solution.py:115
  75.6 2.1 copy.63
  77.7 6.0 %all-to-all-start.3 = ((bf16[2,512,448]{2,0,1:T(2,128)(2,1)}), bf16[2,512,448]{2,0,1:T(2,128)(2,1)}, u32[]{:S(2)}, u32[]{:S(2)}) async-start(bf16[2,512,448]{2,0,1:T(2,128)(2,1)} %copy.63), calls=%async_computation.3 | async-start | bytes 2097152 | tf_op jit(solution)/shard_map/all_to_all | solution.py:116
  83.7 41.3 %all_gather.15 = bf16[128,3584]{0,1:T(8,128)(2,1)S(1)} all-gather(bf16[128,448]{0,1:T(8,128)(2,1)S(1)} %copy.57), channel_id=1, replica_groups=mesh['expert'=64,'replica'=8] {'replica'}, dimensions={1}, use_global_device_ids=true | all-gather | bytes 1032192 | tf_op jit(solution)/shard_map/all_gather | solution.py:80
  125.0 1.1 select_bitcast_fusion.3
  126.1 0.7 copy-done.12
  127.0 1.0 pad_maximum_fusion.2
  128.0 4.3 %copy.69 = bf16[2,64,3584]{1,0,2:T(2,128)(2,1)S(1)} copy(bf16[2,64,3584]{2,1,0:T(8,128)(2,1)} %pad_maximum_fusion.2) | data formatting | bytes 1835008 | tf_op jit(solution)/shard_map/stack | solution.py:20
  132.3 2.1 reshape.363
  134.4 4.2 %all-to-all-start.5 = ((bf16[8,2,28672]{2,1,0:T(2,128)(2,1)}), bf16[8,2,28672]{2,1,0:T(2,128)(2,1)}, u32[]{:S(2)}, u32[]{:S(2)}) async-start(bf16[8,2,28672]{2,1,0:T(2,128)(2,1)} %reshape.363), calls=%async_computation.5 | async-start | bytes 1835008 | tf_op jit(solution)/shard_map/all_to_all | solution.py:130
  138.7 1.2 select_bitcast_fusion.5
  139.9 0.8 copy-done.8
  140.8 1.0 pad_maximum_fusion.1
  141.9 4.3 %copy.66 = bf16[2,64,3584]{1,0,2:T(2,128)(2,1)S(1)} copy(bf16[2,64,3584]{2,1,0:T(8,128)(2,1)} %pad_maximum_fusion.1) | data formatting | bytes 1835008 | tf_op jit(solution)/shard_map/stack | solution.py:20
  146.1 2.1 reshape.365
  148.3 2.2 fusion.9
  150.4 1.4 copy.64
  151.8 0.6 copy.65
  152.4 2.1 all_to_all.57
  154.5 6.7 %all-to-all-start.4 = ((bf16[8,2,28672]{2,1,0:T(2,128)(2,1)}), bf16[8,2,28672]{2,1,0:T(2,128)(2,1)}, u32[]{:S(2)}, u32[]{:S(2)}) async-start(bf16[8,2,28672]{2,1,0:T(2,128)(2,1)} %reshape.365), calls=%async_computation.4 | async-start | bytes 1835008 | tf_op jit(solution)/shard_map/all_to_all | solution.py:129
  161.6 0.6 copy-done.9
  162.8 30.9 %all_gather.16 = bf16[128,2,512]{0,2,1:T(8,128)(2,1)S(1)} all-gather(bf16[128,2,64]{0,2,1:T(8,128)(2,1)S(1)} %get-tuple-element.61), channel_id=1, replica_groups=mesh['expert'=64,'replica'=8] {'replica'}, dimensions={2}, use_global_device_ids=true | all-gather | bytes 294912 | tf_op jit(solution)/shard_map/all_gather | solution.py:98
  194.3 0.7 reshape.212
  195.1 4.5 %reshape.364 = bf16[3584,2,64]{2,1,0:T(2,128)(2,1)S(1)} reshape(bf16[8,2,28672]{2,1,0:T(2,128)(2,1)} %all-to-all-done.5) | data formatting | bytes 1835008
  199.6 3.5 %copy.70 = bf16[2,64,8,448]{3,1,2,0:T(8,128)(2,1)} copy(bf16[2,64,8,448]{1,0,3,2:T(2,128)(2,1)S(1)} %bitcast.164) | data formatting | bytes 1835008 | tf_op jit(solution)/shard_map/all_to_all | solution.py:130
  203.1 18.4 %all_gather.19 = bf16[128,2,512]{0,2,1:T(8,128)(2,1)S(1)} all-gather(bf16[128,2,64]{0,2,1:T(8,128)(2,1)S(1)} %get-tuple-element.60), channel_id=1, replica_groups=mesh['expert'=64,'replica'=8] {'replica'}, dimensions={2}, use_global_device_ids=true | all-gather | bytes 294912 | tf_op jit(solution)/shard_map/all_gather | solution.py:126
  221.5 18.8 %all_gather.18 = bf16[128,2,512]{0,2,1:T(8,128)(2,1)S(1)} all-gather(bf16[128,2,64]{0,2,1:T(8,128)(2,1)S(1)} %get-tuple-element.59), channel_id=1, replica_groups=mesh['expert'=64,'replica'=8] {'replica'}, dimensions={2}, use_global_device_ids=true | all-gather | bytes 294912 | tf_op jit(solution)/shard_map/all_gather | solution.py:125
  240.3 1.7 fusion.7
  242.3 27.9 %all-to-all-start.1 = ((bf16[64,2,448]{2,1,0:T(2,128)(2,1)}), bf16[64,2,448]{2,1,0:T(2,128)(2,1)S(1)}, u32[]{:S(2)}, u32[]{:S(2)}) async-start(bf16[64,2,448]{2,1,0:T(2,128)(2,1)} %reshape.212), calls=%async_computation.1 | async-start | bytes 262144 | tf_op jit(solution)/shard_map/all_to_all | solution.py:103
  270.2 5.3 %reshape.366 = bf16[3584,2,64]{2,1,0:T(2,128)(2,1)} reshape(bf16[8,2,28672]{2,1,0:T(2,128)(2,1)} %all-to-all-done.4) | data formatting | bytes 1835008
  275.5 5.8 %copy.67 = bf16[2,64,8,448]{3,1,2,0:T(8,128)(2,1)} copy(bf16[2,64,8,448]{1,0,3,2:T(2,128)(2,1)} %bitcast.165) | data formatting | bytes 1835008 | tf_op jit(solution)/shard_map/all_to_all | solution.py:129
  281.3 1.8 convolution_bitcast_fusion.1
  283.8 0.7 reshape.216
  284.6 2.3 select_convert_fusion.2
  286.9 2.4 collective-permute-start.3
  289.3 2.0 collective-permute-start.4
  291.3 1.7 fusion.16
  293.0 10.3 %all-to-all-start.6 = ((bf16[64,2,448]{2,1,0:T(2,128)(2,1)}), bf16[64,2,448]{2,1,0:T(2,128)(2,1)S(1)}, u32[]{:S(2)}, u32[]{:S(2)}) async-start(bf16[64,2,448]{2,1,0:T(2,128)(2,1)} %reshape.216), calls=%async_computation.6 | async-start | bytes 262144 | tf_op jit(solution)/shard_map/all_to_all | solution.py:138
  303.3 1.5 select_convert_fusion
  304.8 2.4 collective-permute-start.5
  307.3 0.9 gather_fusion.1
  308.2 5.4 %all-to-all-done.6 = bf16[64,2,448]{2,1,0:T(2,128)(2,1)S(1)} async-done(((bf16[64,2,448]{2,1,0:T(2,128)(2,1)}), bf16[64,2,448]{2,1,0:T(2,128)(2,1)S(1)}, u32[]{:S(2)}, u32[]{:S(2)}) %all-to-all-start.6) | async-done | bytes 114720 | tf_op jit(solution)/shard_map/all_to_all | solution.py:138
  313.8 0.9 gather_fusion.4
  314.7 0.7 bitcast_reduce_fusion
  315.3 0.7 fusion.18
  316.1 2.5 fusion.13
  318.6 2.0 fusion.14
  320.6 2.1 fusion.15
  (84 shorter events, 5.5 us)
Async XLA Ops:
  0.6 10.5 %copy-start = (bf16[12,448]{1,0:T(8,128)(2,1)S(1)}, bf16[12,448]{1,0:T(8,128)(2,1)}, u32[]{:S(2)}) copy-start(bf16[12,448]{1,0:T(8,128)(2,1)} %param.21) | copy-start | bytes 32260
  0.6 27.7 %copy-start.20 = (s32[12,8]{0,1:T(8,128)S(1)}, s32[12,8]{0,1:T(8,128)}, u32[]{:S(2)}) copy-start(s32[12,8]{0,1:T(8,128)} %param.16) | copy-start | bytes 1156
  0.7 23.4 %copy-start.17 = (bf16[1,64,3584]{2,1,0:T(8,128)(2,1)S(1)}, bf16[1,64,3584]{2,1,0:T(8,128)(2,1)}, u32[]{:S(2)}) copy-start(bf16[1,64,3584]{2,1,0:T(8,128)(2,1)} %param.19) | copy-start | bytes 1376260
  0.7 27.7 %copy-start.1 = (bf16[12,448]{1,0:T(8,128)(2,1)S(1)}, bf16[12,448]{1,0:T(8,128)(2,1)}, u32[]{:S(2)}) copy-start(bf16[12,448]{1,0:T(8,128)(2,1)} %param.15) | copy-start | bytes 32260
  0.7 74.7 %collective-permute-start.2 = (bf16[512,448]{0,1:T(8,128)(2,1)}, bf16[512,448]{0,1:T(8,128)(2,1)S(1)}, u32[]{:S(2)}, u32[]{:S(2)}) collective-permute-start(bf16[512,448]{0,1:T(8,128)(2,1)} %bitcast.169), channel_id=1, source_target_pairs={{0,8},{8,0},{16,24},{24,16},{32,40},{40,32},{48,56},{56,48},{64,72... | collective-permute-start | bytes 1376264 | tf_op jit(solution)/shard_map/ppermute | solution.py:14
  13.1 0.6 copy-start.18
  15.9 18.4 %all-to-all-start.2 = ((bf16[64,2,448]{2,1,0:T(2,128)(2,1)}), bf16[64,2,448]{2,1,0:T(2,128)(2,1)S(1)}, u32[]{:S(2)}, u32[]{:S(2)}) async-start(bf16[64,2,448]{2,1,0:T(2,128)(2,1)} %select_convert_fusion.3), calls=%async_computation.2 | async-start | bytes 262144 | tf_op jit(solution)/shard_map/all_to_all | solution.py:63
  24.0 101.0 %collective-permute-start.1 = (bf16[64,3584]{1,0:T(8,128)(2,1)S(1)}, bf16[64,3584]{1,0:T(8,128)(2,1)}, u32[]{:S(2)}, u32[]{:S(2)}) collective-permute-start(bf16[64,3584]{1,0:T(8,128)(2,1)S(1)} %bitcast.170), channel_id=1, source_target_pairs={{0,8},{8,0},{16,24},{24,16},{32,40},{40,32},{48,56},{56,48},{64,72... | collective-permute-start | bytes 1376264 | tf_op jit(solution)/shard_map/ppermute | solution.py:14
  26.4 112.3 %collective-permute-start = (bf16[64,3584]{1,0:T(8,128)(2,1)}, bf16[64,3584]{1,0:T(8,128)(2,1)}, u32[]{:S(2)}, u32[]{:S(2)}) collective-permute-start(bf16[64,3584]{1,0:T(8,128)(2,1)} %bitcast.3), channel_id=1, source_target_pairs={{0,8},{8,0},{16,24},{24,16},{32,40},{40,32},{48,56},{56,48},{64,72... | collective-permute-start | bytes 1376264 | tf_op jit(solution)/shard_map/ppermute | solution.py:14
  28.4 47.0 %copy-start.16 = (bf16[1,512,448]{1,2,0:T(8,128)(2,1)S(1)}, bf16[1,512,448]{1,2,0:T(8,128)(2,1)}, u32[]{:S(2)}) copy-start(bf16[1,512,448]{1,2,0:T(8,128)(2,1)} %param.20) | copy-start | bytes 1376260
  34.4 16.7 %all-to-all-start = ((bf16[64,2,448]{2,1,0:T(2,128)(2,1)}), bf16[64,2,448]{2,1,0:T(2,128)(2,1)S(1)}, u32[]{:S(2)}, u32[]{:S(2)}) async-start(bf16[64,2,448]{2,1,0:T(2,128)(2,1)} %broadcast_select_fusion), calls=%async_computation | async-start | bytes 262144 | tf_op jit(solution)/shard_map/all_to_all | solution.py:56
  75.5 2.2 copy-start.6
  77.7 56.7 %all-to-all-start.3 = ((bf16[2,512,448]{2,0,1:T(2,128)(2,1)}), bf16[2,512,448]{2,0,1:T(2,128)(2,1)}, u32[]{:S(2)}, u32[]{:S(2)}) async-start(bf16[2,512,448]{2,0,1:T(2,128)(2,1)} %copy.63), calls=%async_computation.3 | async-start | bytes 2097152 | tf_op jit(solution)/shard_map/all_to_all | solution.py:116
  126.1 0.8 copy-start.12
  126.1 0.9 copy-start.13
  134.4 20.1 %all-to-all-start.5 = ((bf16[8,2,28672]{2,1,0:T(2,128)(2,1)}), bf16[8,2,28672]{2,1,0:T(2,128)(2,1)}, u32[]{:S(2)}, u32[]{:S(2)}) async-start(bf16[8,2,28672]{2,1,0:T(2,128)(2,1)} %reshape.363), calls=%async_computation.5 | async-start | bytes 1835008 | tf_op jit(solution)/shard_map/all_to_all | solution.py:130
  139.9 0.8 copy-start.8
  139.9 0.9 copy-start.10
  152.4 8.8 %copy-start.4 = (bf16[128,3584]{0,1:T(8,128)(2,1)S(1)}, bf16[128,3584]{0,1:T(8,128)(2,1)}, u32[]{:S(2)}) copy-start(bf16[128,3584]{0,1:T(8,128)(2,1)} %all_gather.17) | copy-start | bytes 2752516
  154.5 6.7 %copy-start.5 = (bf16[2,64,3584]{2,1,0:T(8,128)(2,1)S(1)}, bf16[2,64,3584]{2,1,0:T(8,128)(2,1)}, u32[]{:S(2)}) copy-start(bf16[2,64,3584]{2,1,0:T(8,128)(2,1)} %all_to_all.57) | copy-start | bytes 2752516
  154.5 7.1 %copy-start.21 = (f32[128,2,64]{0,2,1:T(8,128)S(1)}, f32[128,2,64]{0,2,1:T(8,128)}, u32[]{:S(2)}) copy-start(f32[128,2,64]{0,2,1:T(8,128)} %fusion.9) | copy-start | bytes 196612
  154.5 87.8 %all-to-all-start.4 = ((bf16[8,2,28672]{2,1,0:T(2,128)(2,1)}), bf16[8,2,28672]{2,1,0:T(2,128)(2,1)}, u32[]{:S(2)}, u32[]{:S(2)}) async-start(bf16[8,2,28672]{2,1,0:T(2,128)(2,1)} %reshape.365), calls=%async_computation.4 | async-start | bytes 1835008 | tf_op jit(solution)/shard_map/all_to_all | solution.py:129
  161.2 1.0 copy-start.9
  161.2 1.1 copy-start.11
  162.3 31.3 %copy-start.7 = (bf16[1,512,448]{1,2,0:T(8,128)(2,1)S(1)}, bf16[1,512,448]{1,2,0:T(8,128)(2,1)}, u32[]{:S(2)}) copy-start(bf16[1,512,448]{1,2,0:T(8,128)(2,1)} %copy-done.6) | copy-start | bytes 1376260
  193.6 0.7 copy-start.14
  242.3 50.6 %all-to-all-start.1 = ((bf16[64,2,448]{2,1,0:T(2,128)(2,1)}), bf16[64,2,448]{2,1,0:T(2,128)(2,1)S(1)}, u32[]{:S(2)}, u32[]{:S(2)}) async-start(bf16[64,2,448]{2,1,0:T(2,128)(2,1)} %reshape.212), calls=%async_computation.1 | async-start | bytes 262144 | tf_op jit(solution)/shard_map/all_to_all | solution.py:103
  281.3 1.8 copy-start.3
  283.7 7.6 %copy-start.15 = (bf16[128,2,512]{0,2,1:T(8,128)(2,1)S(1)}, bf16[128,2,512]{0,2,1:T(8,128)(2,1)}, u32[]{:S(2)}) copy-start(bf16[128,2,512]{0,2,1:T(8,128)(2,1)} %copy-done.14) | copy-start | bytes 786436
  286.9 29.2 %collective-permute-start.3 = (bf16[64,3584]{1,0:T(8,128)(2,1)}, bf16[64,3584]{1,0:T(8,128)(2,1)}, u32[]{:S(2)}, u32[]{:S(2)}) collective-permute-start(bf16[64,3584]{1,0:T(8,128)(2,1)} %select_convert_fusion.2), channel_id=1, source_target_pairs={{0,8},{8,0},{16,24},{24,16},{32,40},{40,32},{48,56},{56,48},{64,72... | collective-permute-start | bytes 1376264 | tf_op jit(solution)/shard_map/ppermute | solution.py:14
  289.3 29.2 %collective-permute-start.4 = (bf16[64,3584]{1,0:T(8,128)(2,1)S(1)}, bf16[64,3584]{1,0:T(8,128)(2,1)}, u32[]{:S(2)}, u32[]{:S(2)}) collective-permute-start(bf16[64,3584]{1,0:T(8,128)(2,1)S(1)} %select_convert_fusion.1), channel_id=1, source_target_pairs={{0,8},{8,0},{16,24},{24,16},{32,40},{40,32},{48,56},{56,48},{64,72... | collective-permute-start | bytes 1376264 | tf_op jit(solution)/shard_map/ppermute | solution.py:14
  293.0 20.7 %all-to-all-start.6 = ((bf16[64,2,448]{2,1,0:T(2,128)(2,1)}), bf16[64,2,448]{2,1,0:T(2,128)(2,1)S(1)}, u32[]{:S(2)}, u32[]{:S(2)}) async-start(bf16[64,2,448]{2,1,0:T(2,128)(2,1)} %reshape.216), calls=%async_computation.6 | async-start | bytes 262144 | tf_op jit(solution)/shard_map/all_to_all | solution.py:138
  303.3 12.1 %copy-start.19 = (f32[12,8]{1,0:T(8,128)S(1)}, f32[12,8]{1,0:T(8,128)}, u32[]{:S(2)}) copy-start(f32[12,8]{1,0:T(8,128)} %copy-done.18) | copy-start | bytes 1156
  304.8 15.7 %collective-permute-start.5 = (bf16[512,448]{0,1:T(8,128)(2,1)S(1)}, bf16[512,448]{0,1:T(8,128)(2,1)}, u32[]{:S(2)}, u32[]{:S(2)}) collective-permute-start(bf16[512,448]{0,1:T(8,128)(2,1)S(1)} %select_convert_fusion), channel_id=1, source_target_pairs={{0,8},{8,0},{16,24},{24,16},{32,40},{40,32},{48,56},{56,48},{64,72... | collective-permute-start | bytes 1376264 | tf_op jit(solution)/shard_map/ppermute | solution.py:14
  318.6 2.0 copy-start.2
where the time goes:
time: 324 us; the launch traced here: 323 us
  blocking collectives  133 us (41%)
  starting transfers between devices  89.4 us (28%)
  local copies, waits for them, and re-layouts  50.9 us (16%)
  other arithmetic  19.4 us (6%)
  waiting for transfers between devices  18.9 us (6%)
  matrix products  9.43 us (3%)
    all_gather x1, blocking collectives, per_device(): full_rows = lax.all_gather(rows_part, 'replica', axis=1, tiled=True)  41.3 us
    all_gather x1, blocking collectives, per_device(): lax.all_gather(hidden, 'replica', axis=2, tiled=True)  30.9 us
    all_to_all x1, starting transfers between devices, per_device(): lax.all_to_all(expert_out.reshape(experts_axis, capacity, slice_width), '...  27.9 us
    all_gather x1, blocking collectives, per_device(): full_grads = lax.all_gather(grads_part, 'replica', axis=1, tiled=True)  24.1 us
    ppermute x6, starting transfers between devices, partner_2(): return lax.ppermute(block, axis, route)  19.9 us
    unnamed x50, local copies, waits for them, and re-layouts  18.8 us
    all_gather x1, blocking collectives, per_device(): lax.all_gather(gate_act, 'replica', axis=2, tiled=True)  18.8 us
    all_gather x1, blocking collectives, per_device(): lax.all_gather(up_act, 'replica', axis=2, tiled=True)  18.4 us
  transfers between devices with their start and end apart: 13, of which 3 were waited for; matrix products, arithmetic and copies ran while one was open for 22% of the time, Pallas kernels for 0%

commit v1 on v0

--- a/solution.py
+++ b/solution.py
@@ -2,6 +2,24 @@
 import jax.numpy as jnp
 from jax import lax
 from jax.sharding import PartitionSpec as P
+
+
+def ring_gather(value, axis, dim):
+    ways, here, hop = (lax.axis_size(axis), lax.axis_index(axis), value.shape[dim])
+    lengths = [n * ways if d == dim else n for d, n in enumerate(value.shape)]
+    full = lax.dynamic_update_slice_in_dim(
+        jnp.zeros(lengths, value.dtype), value, here * hop, axis=dim
+    )
+    going_up = going_down = value
+    for far in range(1, ways // 2 + 1):
+        going_up = lax.ppermute(going_up, axis, [(d, (d + 1) % ways) for d in range(ways)])
+        full = lax.dynamic_update_slice_in_dim(full, going_up, (here - far) % ways * hop, axis=dim)
+        if 2 * far < ways:
+            going_down = lax.ppermute(going_down, axis, [(d, (d - 1) % ways) for d in range(ways)])
+            full = lax.dynamic_update_slice_in_dim(
+                full, going_down, (here + far) % ways * hop, axis=dim
+            )
+    return full
 
 
 def partner_2(block, axis, distance):
@@ -122,7 +140,7 @@
     gate_local = jnp.einsum("sd,shq->hqd", full_rows, gate_act, preferred_element_type=jnp.float32)
     up_local = jnp.einsum("sd,shq->hqd", full_rows, up_act, preferred_element_type=jnp.float32)
     all_gate_act, all_up_act = (
-        lax.all_gather(gate_act, "replica", axis=2, tiled=True),
+        ring_gather(gate_act, "replica", 2),
         lax.all_gather(up_act, "replica", axis=2, tiled=True),
     )
     rows_gate, rows_up = (

time: 324 us -> 323 us (level)
  blocking collectives: 133 us -> 101 us
  local copies, waits for them, and re-layouts: 50.9 us -> 72.7 us
  starting transfers between devices: 89.4 us -> 110 us
  waiting for transfers between devices: 18.9 us -> 8.68 us
    ppermute x0 -> x7, starting transfers between devices: none -> 22.6 us  [the longest x3 12.1 us: ring_gather(): lax.ppermute(going_down, axis, [(d, (d - 1) % ways) for d in range(ways)])]
    all_gather x1, blocking collectives: 41.3 us -> 21.4 us  [per_device(): full_rows = lax.all_gather(rows_part, 'replica', axis=1, tiled=True)]
    all_gather x1 -> x0, blocking collectives: 18.8 us -> none  [per_device(): lax.all_gather(gate_act, 'replica', axis=2, tiled=True)]
    all_to_all x1, starting transfers between devices: 27.9 us -> 10.2 us  [per_device(): lax.all_to_all(expert_out.reshape(experts_axis, capacity, slice_width), '...]
    ppermute x6, starting transfers between devices: 19.9 us -> 37.2 us  [partner_2(): return lax.ppermute(block, axis, route)]
    ppermute x0 -> x7, local copies, waits for them, and re-layouts: none -> 10.5 us  [the longest x4 5.98 us: ring_gather(): lax.ppermute(going_up, axis, [(d, (d + 1) % ways) for d in range(ways)])]
    dynamic_update_slice x0 -> x8, local copies, waits for them, and re-layouts: none -> 9.86 us  [the longest x4 4.89 us: ring_gather(): lax.dynamic_update_slice_in_dim(full, going_up, (here - far) % ways * hop...]
    all_to_all x1, waiting for transfers between devices: 9.5 us -> 0.01 us  [per_device(): lax.all_to_all(send_rows.reshape(experts_axis, capacity, slice_width), 'e...]
  transfers between devices with their start and end apart: 13 -> 20, of which waited for: 3 -> 2; matrix products, arithmetic and copies ran while one was open for 22% -> 29% of each run, Pallas kernels for 0% -> 0%
where the time goes in v1:
time: 323 us; the launch traced here: 320 us
  starting transfers between devices  110 us (34%)
  blocking collectives  101 us (31%)
  local copies, waits for them, and re-layouts  72.7 us (23%)
  other arithmetic  17.3 us (5%)
  waiting for transfers between devices  8.68 us (3%)
  matrix products  8.39 us (3%)
    ppermute x6, starting transfers between devices, partner_2(): return lax.ppermute(block, axis, route)  37.2 us
    all_gather x1, blocking collectives, per_device(): lax.all_gather(up_act, 'replica', axis=2, tiled=True)  27.5 us
    all_gather x1, blocking collectives, per_device(): lax.all_gather(hidden, 'replica', axis=2, tiled=True)  27.3 us
    all_gather x1, blocking collectives, per_device(): full_grads = lax.all_gather(grads_part, 'replica', axis=1, tiled=True)  25.2 us
    all_gather x1, blocking collectives, per_device(): full_rows = lax.all_gather(rows_part, 'replica', axis=1, tiled=True)  21.4 us
    unnamed x42, local copies, waits for them, and re-layouts  19.1 us
    ppermute x3, starting transfers between devices, ring_gather(): lax.ppermute(going_down, axis, [(d, (d - 1) % ways) for d in range(ways)])  12.1 us
    another operation x3, local copies, waits for them, and re-layouts, pair_join(): return jnp.stack([first_part, second_part], axis=stack_axis)  10.7 us
  transfers between devices with their start and end apart: 20, of which 2 were waited for; matrix products, arithmetic and copies ran while one was open for 29% of the time, Pallas kernels for 0%

profile of v1, /device:TPU:1, one launch (start us, length us, event | category | flops | bytes accessed | tf_op | source)
XLA Modules:
  0.0 320.0 jit_solution(14434816095217856506)
XLA Ops:
  0.7 8.9 %collective-permute-start.2 = (bf16[512,448]{0,1:T(8,128)(2,1)}, bf16[512,448]{0,1:T(8,128)(2,1)S(1)}, u32[]{:S(2)}, u32[]{:S(2)}) collective-permute-start(bf16[512,448]{0,1:T(8,128)(2,1)} %bitcast.169), channel_id=1, source_target_pairs={{0,8},{8,0},{16,24},{24,16},{32,40},{40,32},{48,56},{56,48},{64,72... | collective-permute-start | bytes 1376264 | tf_op jit(solution)/shard_map/ppermute | solution.py:32
  13.2 1.2 gather_fusion.2
  15.4 8.1 %all-to-all-start.2 = ((bf16[64,2,448]{2,1,0:T(2,128)(2,1)}), bf16[64,2,448]{2,1,0:T(2,128)(2,1)S(1)}, u32[]{:S(2)}, u32[]{:S(2)}) async-start(bf16[64,2,448]{2,1,0:T(2,128)(2,1)} %select_convert_fusion.3), calls=%async_computation.2 | async-start | bytes 262144 | tf_op jit(solution)/shard_map/all_to_all | solution.py:81
  23.5 2.4 collective-permute-start.1
  25.9 2.0 collective-permute-start
  30.0 3.8 %all-to-all-done.2 = bf16[64,2,448]{2,1,0:T(2,128)(2,1)S(1)} async-done(((bf16[64,2,448]{2,1,0:T(2,128)(2,1)}), bf16[64,2,448]{2,1,0:T(2,128)(2,1)S(1)}, u32[]{:S(2)}, u32[]{:S(2)}) %all-to-all-start.2) | async-done | bytes 114720 | tf_op jit(solution)/shard_map/all_to_all | solution.py:81
  33.9 6.5 %all-to-all-start = ((bf16[64,2,448]{2,1,0:T(2,128)(2,1)}), bf16[64,2,448]{2,1,0:T(2,128)(2,1)S(1)}, u32[]{:S(2)}, u32[]{:S(2)}) async-start(bf16[64,2,448]{2,1,0:T(2,128)(2,1)} %broadcast_select_fusion), calls=%async_computation | async-start | bytes 262144 | tf_op jit(solution)/shard_map/all_to_all | solution.py:74
  40.6 25.2 %all_gather.14 = bf16[128,3584]{0,1:T(8,128)(2,1)} all-gather(bf16[128,448]{0,1:T(8,128)(2,1)S(1)} %copy.86), channel_id=1, replica_groups=mesh['expert'=64,'replica'=8] {'replica'}, dimensions={1}, use_global_device_ids=true | all-gather | bytes 1032192 | tf_op jit(solution)/shard_map/all_gather | solution.py:133
  66.0 21.4 %all_gather.12 = bf16[128,3584]{0,1:T(8,128)(2,1)S(1)} all-gather(bf16[128,448]{0,1:T(8,128)(2,1)S(1)} %copy.81), channel_id=1, replica_groups=mesh['expert'=64,'replica'=8] {'replica'}, dimensions={1}, use_global_device_ids=true | all-gather | bytes 1032192 | tf_op jit(solution)/shard_map/all_gather | solution.py:98
  87.7 2.1 copy.87
  89.7 4.2 %all-to-all-start.3 = ((bf16[2,512,448]{2,0,1:T(2,128)(2,1)}), bf16[2,512,448]{2,0,1:T(2,128)(2,1)}, u32[]{:S(2)}, u32[]{:S(2)}) async-start(bf16[2,512,448]{2,0,1:T(2,128)(2,1)} %copy.87), calls=%async_computation.3 | async-start | bytes 2097152 | tf_op jit(solution)/shard_map/all_to_all | solution.py:134
  94.0 1.2 select_bitcast_fusion.3
  96.2 1.0 pad_maximum_fusion.2
  97.2 4.3 %copy.101 = bf16[2,64,3584]{1,0,2:T(2,128)(2,1)S(1)} copy(bf16[2,64,3584]{2,1,0:T(8,128)(2,1)} %pad_maximum_fusion.2) | data formatting | bytes 1835008 | tf_op jit(solution)/shard_map/stack | solution.py:38
  101.5 2.1 reshape.363
  103.6 1.2 select_bitcast_fusion.5
  105.7 1.0 pad_maximum_fusion.1
  106.7 4.3 %copy.98 = bf16[2,64,3584]{1,0,2:T(2,128)(2,1)S(1)} copy(bf16[2,64,3584]{2,1,0:T(8,128)(2,1)} %pad_maximum_fusion.1) | data formatting | bytes 1835008 | tf_op jit(solution)/shard_map/stack | solution.py:38
  111.0 2.1 reshape.365
  113.2 1.5 fusion.9
  114.7 6.6 %all-to-all-start.5 = ((bf16[8,2,28672]{2,1,0:T(2,128)(2,1)}), bf16[8,2,28672]{2,1,0:T(2,128)(2,1)}, u32[]{:S(2)}, u32[]{:S(2)}) async-start(bf16[8,2,28672]{2,1,0:T(2,128)(2,1)} %reshape.363), calls=%async_computation.5 | async-start | bytes 1835008 | tf_op jit(solution)/shard_map/all_to_all | solution.py:148
  121.4 1.4 copy.88
  123.4 2.1 all_to_all.57
  125.5 1.9 fusion.3
  127.8 3.4 %collective-permute-start.3 = (bf16[128,2,64]{0,2,1:T(8,128)(2,1)S(1)}, bf16[128,2,64]{0,2,1:T(8,128)(2,1)S(1)}, u32[]{:S(2)}, u32[]{:S(2)}) collective-permute-start(bf16[128,2,64]{0,2,1:T(8,128)(2,1)S(1)} %get-tuple-element.59), channel_id=1, source_target_pairs={{0,1},{1,2},{2,3},{3,4},{4,5},{5,6},{6,7},{7,0},{8,9},{9,10},{10,1... | collective-permute-start | bytes 98312 | tf_op jit(solution)/shard_map/ppermute | solution.py:15
  131.2 3.1 collective-permute-start.4
  134.3 27.3 %all_gather.13 = bf16[128,2,512]{0,2,1:T(8,128)(2,1)} all-gather(bf16[128,2,64]{0,2,1:T(8,128)(2,1)S(1)} %get-tuple-element.61), channel_id=1, replica_groups=mesh['expert'=64,'replica'=8] {'replica'}, dimensions={2}, use_global_device_ids=true | all-gather | bytes 294912 | tf_op jit(solution)/shard_map/all_gather | solution.py:116
  164.2 4.4 %all-to-all-start.4 = ((bf16[8,2,28672]{2,1,0:T(2,128)(2,1)}), bf16[8,2,28672]{2,1,0:T(2,128)(2,1)}, u32[]{:S(2)}, u32[]{:S(2)}) async-start(bf16[8,2,28672]{2,1,0:T(2,128)(2,1)} %reshape.365), calls=%async_computation.4 | async-start | bytes 1835008 | tf_op jit(solution)/shard_map/all_to_all | solution.py:147
  168.6 1.7 fusion.16
  170.7 3.2 %collective-permute-start.5 = (bf16[128,2,64]{0,2,1:T(8,128)(2,1)S(1)}, bf16[128,2,64]{0,2,1:T(8,128)(2,1)S(1)}, u32[]{:S(2)}, u32[]{:S(2)}) collective-permute-start(bf16[128,2,64]{0,2,1:T(8,128)(2,1)S(1)} %collective-permute-done.3), channel_id=1, source_target_pairs={{0,1},{1,2},{2,3},{3,4},{4,5},{5,6},{6,7},{7,0},{8,9},{9,10},{10,1... | collective-permute-start | bytes 98312 | tf_op jit(solution)/shard_map/ppermute | solution.py:15
  173.9 27.5 %all_gather.15 = bf16[128,2,512]{0,2,1:T(8,128)(2,1)S(1)} all-gather(bf16[128,2,64]{0,2,1:T(8,128)(2,1)S(1)} %get-tuple-element.60), channel_id=1, replica_groups=mesh['expert'=64,'replica'=8] {'replica'}, dimensions={2}, use_global_device_ids=true | all-gather | bytes 294912 | tf_op jit(solution)/shard_map/all_gather | solution.py:144
  202.3 5.3 %reshape.364 = bf16[3584,2,64]{2,1,0:T(2,128)(2,1)} reshape(bf16[8,2,28672]{2,1,0:T(2,128)(2,1)} %all-to-all-done.5) | data formatting | bytes 1835008
  207.6 4.6 %copy.102 = bf16[2,64,8,448]{3,1,2,0:T(8,128)(2,1)S(1)} copy(bf16[2,64,8,448]{1,0,3,2:T(2,128)(2,1)} %bitcast.164) | data formatting | bytes 1835008 | tf_op jit(solution)/shard_map/all_to_all | solution.py:148
  212.2 19.4 %collective-permute-start.10 = (bf16[64,3584]{1,0:T(8,128)(2,1)}, bf16[64,3584]{1,0:T(8,128)(2,1)}, u32[]{:S(2)}, u32[]{:S(2)}) collective-permute-start(bf16[64,3584]{1,0:T(8,128)(2,1)} %select_convert_fusion.2), channel_id=1, source_target_pairs={{0,8},{8,0},{16,24},{24,16},{32,40},{40,32},{48,56},{56,48},{64,72... | collective-permute-start | bytes 1376264 | tf_op jit(solution)/shard_map/ppermute | solution.py:32
  231.6 4.1 %collective-permute-start.6 = (bf16[128,2,64]{0,2,1:T(8,128)(2,1)S(1)}, bf16[128,2,64]{0,2,1:T(8,128)(2,1)}, u32[]{:S(2)}, u32[]{:S(2)}) collective-permute-start(bf16[128,2,64]{0,2,1:T(8,128)(2,1)S(1)} %collective-permute-done.4), channel_id=1, source_target_pairs={{0,7},{1,0},{2,1},{3,2},{4,3},{5,4},{6,5},{7,6},{8,15},{9,8},{10,9... | collective-permute-start | bytes 98312 | tf_op jit(solution)/shard_map/ppermute | solution.py:18
  235.8 1.9 collective-permute-start.7
  238.6 2.2 collective-permute-start.11
  240.8 4.9 %collective-permute-start.8 = (bf16[128,2,64]{0,2,1:T(8,128)(2,1)}, bf16[128,2,64]{0,2,1:T(8,128)(2,1)}, u32[]{:S(2)}, u32[]{:S(2)}) collective-permute-start(bf16[128,2,64]{0,2,1:T(8,128)(2,1)} %collective-permute-done.6), channel_id=1, source_target_pairs={{0,7},{1,0},{2,1},{3,2},{4,3},{5,4},{6,5},{7,6},{8,15},{9,8},{10,9... | collective-permute-start | bytes 98312 | tf_op jit(solution)/shard_map/ppermute | solution.py:18
  245.7 1.9 collective-permute-start.9
  248.9 10.2 %all-to-all-start.1 = ((bf16[64,2,448]{2,1,0:T(2,128)(2,1)}), bf16[64,2,448]{2,1,0:T(2,128)(2,1)S(1)}, u32[]{:S(2)}, u32[]{:S(2)}) async-start(bf16[64,2,448]{2,1,0:T(2,128)(2,1)} %reshape.212), calls=%async_computation.1 | async-start | bytes 262144 | tf_op jit(solution)/shard_map/all_to_all | solution.py:121
  259.0 5.3 %reshape.366 = bf16[3584,2,64]{2,1,0:T(2,128)(2,1)} reshape(bf16[8,2,28672]{2,1,0:T(2,128)(2,1)} %all-to-all-done.4) | data formatting | bytes 1835008
  264.3 4.6 %copy.99 = bf16[2,64,8,448]{3,1,2,0:T(8,128)(2,1)S(1)} copy(bf16[2,64,8,448]{1,0,3,2:T(2,128)(2,1)} %bitcast.165) | data formatting | bytes 1835008 | tf_op jit(solution)/shard_map/all_to_all | solution.py:147
  269.0 1.1 dynamic_update_slice.24
  270.0 1.5 copy.91
  271.5 1.4 dynamic_update_slice.25
  272.9 1.5 copy.92
  274.4 1.4 dynamic_update_slice.26
  275.9 1.5 copy.93
  278.4 1.5 copy.94
  279.9 1.0 dynamic_update_slice.28
  280.9 1.5 copy.95
  282.4 1.4 dynamic_update_slice.29
  283.9 1.5 copy.96
  285.4 1.4 dynamic_update_slice.30
  286.8 1.5 copy.97
  288.3 1.0 dynamic_update_slice.31
  289.4 1.1 fusion.1
  292.2 10.3 %all-to-all-start.6 = ((bf16[64,2,448]{2,1,0:T(2,128)(2,1)}), bf16[64,2,448]{2,1,0:T(2,128)(2,1)S(1)}, u32[]{:S(2)}, u32[]{:S(2)}) async-start(bf16[64,2,448]{2,1,0:T(2,128)(2,1)} %reshape.216), calls=%async_computation.6 | async-start | bytes 262144 | tf_op jit(solution)/shard_map/all_to_all | solution.py:156
  302.5 1.5 select_convert_fusion
  304.1 2.4 collective-permute-start.12
  308.1 4.8 %all-to-all-done.6 = bf16[64,2,448]{2,1,0:T(2,128)(2,1)S(1)} async-done(((bf16[64,2,448]{2,1,0:T(2,128)(2,1)}), bf16[64,2,448]{2,1,0:T(2,128)(2,1)S(1)}, u32[]{:S(2)}, u32[]{:S(2)}) %all-to-all-start.6) | async-done | bytes 114720 | tf_op jit(solution)/shard_map/all_to_all | solution.py:156
  314.5 2.5 fusion.13
  316.9 2.0 fusion.14
  319.0 1.1 fusion.15
  (106 shorter events, 21.8 us)
Async XLA Ops:
  0.6 10.5 %copy-start = (bf16[12,448]{1,0:T(8,128)(2,1)S(1)}, bf16[12,448]{1,0:T(8,128)(2,1)}, u32[]{:S(2)}) copy-start(bf16[12,448]{1,0:T(8,128)(2,1)} %param.21) | copy-start | bytes 32260
  0.6 27.2 %copy-start.17 = (s32[12,8]{0,1:T(8,128)S(1)}, s32[12,8]{0,1:T(8,128)}, u32[]{:S(2)}) copy-start(s32[12,8]{0,1:T(8,128)} %param.16) | copy-start | bytes 1156
  0.7 27.3 %copy-start.1 = (bf16[12,448]{1,0:T(8,128)(2,1)S(1)}, bf16[12,448]{1,0:T(8,128)(2,1)}, u32[]{:S(2)}) copy-start(bf16[12,448]{1,0:T(8,128)(2,1)} %param.15) | copy-start | bytes 32260
  0.7 86.8 %collective-permute-start.2 = (bf16[512,448]{0,1:T(8,128)(2,1)}, bf16[512,448]{0,1:T(8,128)(2,1)S(1)}, u32[]{:S(2)}, u32[]{:S(2)}) collective-permute-start(bf16[512,448]{0,1:T(8,128)(2,1)} %bitcast.169), channel_id=1, source_target_pairs={{0,8},{8,0},{16,24},{24,16},{32,40},{40,32},{48,56},{56,48},{64,72... | collective-permute-start | bytes 1376264 | tf_op jit(solution)/shard_map/ppermute | solution.py:32
  15.4 18.4 %all-to-all-start.2 = ((bf16[64,2,448]{2,1,0:T(2,128)(2,1)}), bf16[64,2,448]{2,1,0:T(2,128)(2,1)S(1)}, u32[]{:S(2)}, u32[]{:S(2)}) async-start(bf16[64,2,448]{2,1,0:T(2,128)(2,1)} %select_convert_fusion.3), calls=%async_computation.2 | async-start | bytes 262144 | tf_op jit(solution)/shard_map/all_to_all | solution.py:81
  23.5 70.5 %collective-permute-start.1 = (bf16[64,3584]{1,0:T(8,128)(2,1)}, bf16[64,3584]{1,0:T(8,128)(2,1)}, u32[]{:S(2)}, u32[]{:S(2)}) collective-permute-start(bf16[64,3584]{1,0:T(8,128)(2,1)} %bitcast.6), channel_id=1, source_target_pairs={{0,8},{8,0},{16,24},{24,16},{32,40},{40,32},{48,56},{56,48},{64,72... | collective-permute-start | bytes 1376264 | tf_op jit(solution)/shard_map/ppermute | solution.py:32
  25.9 77.7 %collective-permute-start = (bf16[64,3584]{1,0:T(8,128)(2,1)}, bf16[64,3584]{1,0:T(8,128)(2,1)}, u32[]{:S(2)}, u32[]{:S(2)}) collective-permute-start(bf16[64,3584]{1,0:T(8,128)(2,1)} %bitcast.3), channel_id=1, source_target_pairs={{0,8},{8,0},{16,24},{24,16},{32,40},{40,32},{48,56},{56,48},{64,72... | collective-permute-start | bytes 1376264 | tf_op jit(solution)/shard_map/ppermute | solution.py:32
  28.9 58.5 %copy-start.13 = (bf16[1,512,448]{1,2,0:T(8,128)(2,1)S(1)}, bf16[1,512,448]{1,2,0:T(8,128)(2,1)}, u32[]{:S(2)}) copy-start(bf16[1,512,448]{1,2,0:T(8,128)(2,1)} %param.20) | copy-start | bytes 1376260
  33.9 31.9 %all-to-all-start = ((bf16[64,2,448]{2,1,0:T(2,128)(2,1)}), bf16[64,2,448]{2,1,0:T(2,128)(2,1)S(1)}, u32[]{:S(2)}, u32[]{:S(2)}) async-start(bf16[64,2,448]{2,1,0:T(2,128)(2,1)} %broadcast_select_fusion), calls=%async_computation | async-start | bytes 262144 | tf_op jit(solution)/shard_map/all_to_all | solution.py:74
  87.5 2.2 copy-start.4
  89.7 25.0 %all-to-all-start.3 = ((bf16[2,512,448]{2,0,1:T(2,128)(2,1)}), bf16[2,512,448]{2,0,1:T(2,128)(2,1)}, u32[]{:S(2)}, u32[]{:S(2)}) async-start(bf16[2,512,448]{2,0,1:T(2,128)(2,1)} %copy.87), calls=%async_computation.3 | async-start | bytes 2097152 | tf_op jit(solution)/shard_map/all_to_all | solution.py:134
  95.2 0.8 copy-start.10
  95.2 0.9 copy-start.11
  104.8 0.8 copy-start.6
  104.8 0.9 copy-start.8
  114.7 49.5 %all-to-all-start.5 = ((bf16[8,2,28672]{2,1,0:T(2,128)(2,1)}), bf16[8,2,28672]{2,1,0:T(2,128)(2,1)}, u32[]{:S(2)}, u32[]{:S(2)}) async-start(bf16[8,2,28672]{2,1,0:T(2,128)(2,1)} %reshape.363), calls=%async_computation.5 | async-start | bytes 1835008 | tf_op jit(solution)/shard_map/all_to_all | solution.py:148
  123.3 4.0 %copy-start.7 = (bf16[1,64,3584]{2,1,0:T(8,128)(2,1)S(1)}, bf16[1,64,3584]{2,1,0:T(8,128)(2,1)}, u32[]{:S(2)}) copy-start(bf16[1,64,3584]{2,1,0:T(8,128)(2,1)} %copy-done.6) | copy-start | bytes 1376260
  125.4 1.9 copy-start.9
  127.8 42.8 %collective-permute-start.3 = (bf16[128,2,64]{0,2,1:T(8,128)(2,1)S(1)}, bf16[128,2,64]{0,2,1:T(8,128)(2,1)S(1)}, u32[]{:S(2)}, u32[]{:S(2)}) collective-permute-start(bf16[128,2,64]{0,2,1:T(8,128)(2,1)S(1)} %get-tuple-element.59), channel_id=1, source_target_pairs={{0,1},{1,2},{2,3},{3,4},{4,5},{5,6},{6,7},{7,0},{8,9},{9,10},{10,1... | collective-permute-start | bytes 98312 | tf_op jit(solution)/shard_map/ppermute | solution.py:15
  131.2 100.4 %collective-permute-start.4 = (bf16[128,2,64]{0,2,1:T(8,128)(2,1)S(1)}, bf16[128,2,64]{0,2,1:T(8,128)(2,1)S(1)}, u32[]{:S(2)}, u32[]{:S(2)}) collective-permute-start(bf16[128,2,64]{0,2,1:T(8,128)(2,1)S(1)} %get-tuple-element.59), channel_id=1, source_target_pairs={{0,7},{1,0},{2,1},{3,2},{4,3},{5,4},{6,5},{7,6},{8,15},{9,8},{10,9... | collective-permute-start | bytes 98312 | tf_op jit(solution)/shard_map/ppermute | solution.py:18
  162.1 1.3 copy-start.2
  163.3 5.2 %copy-start.12 = (bf16[128,2,512]{0,2,1:T(8,128)(2,1)S(1)}, bf16[128,2,512]{0,2,1:T(8,128)(2,1)}, u32[]{:S(2)}) copy-start(bf16[128,2,512]{0,2,1:T(8,128)(2,1)} %all_gather.13) | copy-start | bytes 786436
  164.2 6.1 %copy-start.5 = (bf16[1,512,448]{1,2,0:T(8,128)(2,1)S(1)}, bf16[1,512,448]{1,2,0:T(8,128)(2,1)}, u32[]{:S(2)}) copy-start(bf16[1,512,448]{1,2,0:T(8,128)(2,1)} %copy-done.4) | copy-start | bytes 1376260
  164.2 84.7 %all-to-all-start.4 = ((bf16[8,2,28672]{2,1,0:T(2,128)(2,1)}), bf16[8,2,28672]{2,1,0:T(2,128)(2,1)}, u32[]{:S(2)}, u32[]{:S(2)}) async-start(bf16[8,2,28672]{2,1,0:T(2,128)(2,1)} %reshape.365), calls=%async_computation.4 | async-start | bytes 1835008 | tf_op jit(solution)/shard_map/all_to_all | solution.py:147
  170.7 41.5 %copy-start.15 = (bf16[128,2,64]{0,2,1:T(8,128)(2,1)}, bf16[128,2,64]{0,2,1:T(8,128)(2,1)S(1)}, u32[]{:S(2)}) copy-start(bf16[128,2,64]{0,2,1:T(8,128)(2,1)S(1)} %collective-permute-done.3) | copy-start | bytes 98308
  170.7 65.1 %collective-permute-start.5 = (bf16[128,2,64]{0,2,1:T(8,128)(2,1)S(1)}, bf16[128,2,64]{0,2,1:T(8,128)(2,1)S(1)}, u32[]{:S(2)}, u32[]{:S(2)}) collective-permute-start(bf16[128,2,64]{0,2,1:T(8,128)(2,1)S(1)} %collective-permute-done.3), channel_id=1, source_target_pairs={{0,1},{1,2},{2,3},{3,4},{4,5},{5,6},{6,7},{7,0},{8,9},{9,10},{10,1... | collective-permute-start | bytes 98312 | tf_op jit(solution)/shard_map/ppermute | solution.py:15
  212.2 102.3 %collective-permute-start.10 = (bf16[64,3584]{1,0:T(8,128)(2,1)}, bf16[64,3584]{1,0:T(8,128)(2,1)}, u32[]{:S(2)}, u32[]{:S(2)}) collective-permute-start(bf16[64,3584]{1,0:T(8,128)(2,1)} %select_convert_fusion.2), channel_id=1, source_target_pairs={{0,8},{8,0},{16,24},{24,16},{32,40},{40,32},{48,56},{56,48},{64,72... | collective-permute-start | bytes 1376264 | tf_op jit(solution)/shard_map/ppermute | solution.py:32
  231.6 17.2 %copy-start.14 = (bf16[128,2,64]{0,2,1:T(8,128)(2,1)}, bf16[128,2,64]{0,2,1:T(8,128)(2,1)S(1)}, u32[]{:S(2)}) copy-start(bf16[128,2,64]{0,2,1:T(8,128)(2,1)S(1)} %collective-permute-done.4) | copy-start | bytes 98308
  231.6 9.1 %collective-permute-start.6 = (bf16[128,2,64]{0,2,1:T(8,128)(2,1)S(1)}, bf16[128,2,64]{0,2,1:T(8,128)(2,1)}, u32[]{:S(2)}, u32[]{:S(2)}) collective-permute-start(bf16[128,2,64]{0,2,1:T(8,128)(2,1)S(1)} %collective-permute-done.4), channel_id=1, source_target_pairs={{0,7},{1,0},{2,1},{3,2},{4,3},{5,4},{6,5},{7,6},{8,15},{9,8},{10,9... | collective-permute-start | bytes 98312 | tf_op jit(solution)/shard_map/ppermute | solution.py:18
  235.8 13.1 %copy-start.16 = (bf16[128,2,64]{0,2,1:T(8,128)(2,1)}, bf16[128,2,64]{0,2,1:T(8,128)(2,1)S(1)}, u32[]{:S(2)}) copy-start(bf16[128,2,64]{0,2,1:T(8,128)(2,1)S(1)} %collective-permute-done.5) | copy-start | bytes 98308
  235.8 9.9 %collective-permute-start.7 = (bf16[128,2,64]{0,2,1:T(8,128)(2,1)S(1)}, bf16[128,2,64]{0,2,1:T(8,128)(2,1)}, u32[]{:S(2)}, u32[]{:S(2)}) collective-permute-start(bf16[128,2,64]{0,2,1:T(8,128)(2,1)S(1)} %collective-permute-done.5), channel_id=1, source_target_pairs={{0,1},{1,2},{2,3},{3,4},{4,5},{5,6},{6,7},{7,0},{8,9},{9,10},{10,1... | collective-permute-start | bytes 98312 | tf_op jit(solution)/shard_map/ppermute | solution.py:15
  238.6 78.4 %collective-permute-start.11 = (bf16[64,3584]{1,0:T(8,128)(2,1)}, bf16[64,3584]{1,0:T(8,128)(2,1)}, u32[]{:S(2)}, u32[]{:S(2)}) collective-permute-start(bf16[64,3584]{1,0:T(8,128)(2,1)} %select_convert_fusion.1), channel_id=1, source_target_pairs={{0,8},{8,0},{16,24},{24,16},{32,40},{40,32},{48,56},{56,48},{64,72... | collective-permute-start | bytes 1376264 | tf_op jit(solution)/shard_map/ppermute | solution.py:32
  240.8 43.1 %collective-permute-start.8 = (bf16[128,2,64]{0,2,1:T(8,128)(2,1)}, bf16[128,2,64]{0,2,1:T(8,128)(2,1)}, u32[]{:S(2)}, u32[]{:S(2)}) collective-permute-start(bf16[128,2,64]{0,2,1:T(8,128)(2,1)} %collective-permute-done.6), channel_id=1, source_target_pairs={{0,7},{1,0},{2,1},{3,2},{4,3},{5,4},{6,5},{7,6},{8,15},{9,8},{10,9... | collective-permute-start | bytes 98312 | tf_op jit(solution)/shard_map/ppermute | solution.py:18
  245.7 41.2 %collective-permute-start.9 = (bf16[128,2,64]{0,2,1:T(8,128)(2,1)}, bf16[128,2,64]{0,2,1:T(8,128)(2,1)}, u32[]{:S(2)}, u32[]{:S(2)}) collective-permute-start(bf16[128,2,64]{0,2,1:T(8,128)(2,1)} %collective-permute-done.7), channel_id=1, source_target_pairs={{0,1},{1,2},{2,3},{3,4},{4,5},{5,6},{6,7},{7,0},{8,9},{9,10},{10,1... | collective-permute-start | bytes 98312 | tf_op jit(solution)/shard_map/ppermute | solution.py:15
  248.9 43.4 %all-to-all-start.1 = ((bf16[64,2,448]{2,1,0:T(2,128)(2,1)}), bf16[64,2,448]{2,1,0:T(2,128)(2,1)S(1)}, u32[]{:S(2)}, u32[]{:S(2)}) async-start(bf16[64,2,448]{2,1,0:T(2,128)(2,1)} %reshape.212), calls=%async_computation.1 | async-start | bytes 262144 | tf_op jit(solution)/shard_map/all_to_all | solution.py:121
  292.2 20.7 %all-to-all-start.6 = ((bf16[64,2,448]{2,1,0:T(2,128)(2,1)}), bf16[64,2,448]{2,1,0:T(2,128)(2,1)S(1)}, u32[]{:S(2)}, u32[]{:S(2)}) async-start(bf16[64,2,448]{2,1,0:T(2,128)(2,1)} %reshape.216), calls=%async_computation.6 | async-start | bytes 262144 | tf_op jit(solution)/shard_map/all_to_all | solution.py:156
  304.1 14.9 %collective-permute-start.12 = (bf16[512,448]{0,1:T(8,128)(2,1)S(1)}, bf16[512,448]{0,1:T(8,128)(2,1)S(1)}, u32[]{:S(2)}, u32[]{:S(2)}) collective-permute-start(bf16[512,448]{0,1:T(8,128)(2,1)S(1)} %select_convert_fusion), channel_id=1, source_target_pairs={{0,8},{8,0},{16,24},{24,16},{32,40},{40,32},{48,56},{56,48},{64,72... | collective-permute-start | bytes 1376264 | tf_op jit(solution)/shard_map/ppermute | solution.py:32
  316.9 2.0 copy-start.3
